TPU v7x, 256 devices: a whole 4x4x8 slice. The times are simulated.
256 devices in a mesh: group: 4 (over x), img: 32 (over z, y), tensor: 2 (over core).
Axes of the slice: x: 4, y: 4, z: 8, core: 2. Of those that a mesh axis runs over, the one named last changes fastest.
Arguments:
- features: bfloat16 [8, 4096, 8192], P('group', ('img', 'tensor')), may hold values from -6 to 6
- kv_weights: bfloat16 [2, 8192, 1024], P(None, 'img', 'tensor'), may hold values from -0.0625 to 0.0625
- key_gain: float32 [128], replicated, may hold values from 0.1 to 1.9
- queries: bfloat16 [1536, 8192], P('group', 'tensor'), may hold values from -70 to 70
- out_weight: bfloat16 [8192, 8192], P('tensor', 'img'), may hold values from -6 to 6
- attn_gate: float32 [1], replicated, may hold values from 0.4 to 1.5
- group_images: int32 [4, 2], replicated, may hold values from 0 to 7, as said below
- tile_valid: int32 [8, 4], replicated, may hold values from 1 to 1024
Outputs:
- gated: bfloat16 [1536, 8192], P(('group', 'tensor'), 'img')
Inputs may be any that keep to these rules, and one draw needn't show every extreme that they name: `group_images`: every image appears exactly once. Image e is encoded at encoder index e // 2, and one group's images come from different encoder indices.
All inputs are finite; a program needn't handle non-finite values.
Results may differ from a plain program's by a relative error of at most 0.029.
Values may be sent and summed in bfloat16 or wider, within the bound.
A program may use at most 128 MiB of HBM per device.

v0:
```python
import math

import jax
import jax.numpy as jnp
from jax import lax
from jax.experimental import pallas as pl
from jax.experimental.pallas import tpu as pltpu
from jax.sharding import PartitionSpec as P

HD = 128
MESH = pl.DeviceIdType.MESH
BF = jnp.bfloat16
F32 = jnp.float32
NX, NY, NZ = 4, 4, 8
WIDE = 512
NARROW = 1024 - WIDE


def fused(
    feat, kvw, gain, queries, out_w, gate, images_hbm, counts_hbm, out,
    images, counts, a_ref, w_ref, p_ref, rs_relay, rs_recv, xs_ref, xk_ref, xv_ref, ks_ref, vs_ref, kb_ref, vb_ref,
    q_ref, pr_ref, o_ref, st_ref, zo_ref, zs_ref, at1, at2, ow_ref, acc_ref, cs_ref, cr_ref,
    loc_sem, f_send, f_recv, c_fsend, c_frecv, w_send, w_recv, wx_send, wx_recv,
    rs_send, rs_rsem, x_send, x_recv, pair_send, pair_recv, zo_send, zo_recv, zs_send, zs_recv,
    y2_send, y2_recv, z1_send, z1_recv, z2_send, z2_recv, y1_send, y1_recv, c_send, c_recv,
):
    x = lax.axis_index("group")
    img = lax.axis_index("img")
    t = lax.axis_index("tensor")
    z = img // NY
    y = img % NY
    other = 1 - t
    slot = z % 2

    def ym(d):
        return (y + d + NY) % NY

    def zm(d):
        return (z + d + NZ) % NZ

    def xm(d):
        return (x + d + NX) % NX

    def to_y(d):
        return {"img": z * NY + ym(d)}

    def to_z(d):
        return {"img": zm(d) * NY + y}

    def to_x(d):
        return {"group": xm(d)}

    sibling = {"tensor": other}
    partner = {"img": (z + 1 - 2 * slot) * NY + y}
    sends = []

    def remote(src, dst, ssem, rsem, where):
        return pltpu.make_async_remote_copy(
            src_ref=src, dst_ref=dst, send_sem=ssem, recv_sem=rsem,
            device_id=where, device_id_type=MESH,
        )

    def send(src, dst, ssem, rsem, where):
        copy = remote(src, dst, ssem, rsem, where)
        copy.start()
        sends.append(copy)

    def arrived(ref, sem):
        pltpu.make_async_copy(ref, ref, sem).wait()

    locals_ = []

    def fetch(src, dst, sem):
        copy = pltpu.make_async_copy(src, dst, sem)
        copy.start()
        locals_.append(copy)

    third = (
        pl.ds(pl.multiple_of(128 + x * 32, 32), 32),
        pl.ds(pl.multiple_of(128 + x * 32, 16), 16),
        pl.ds(pl.multiple_of(128 + x * 32 + 16, 16), 16),
    )

    def columns(block, kind):
        return pl.ds(pl.multiple_of((block * NY + kind) * 256, 256), 256)

    def place(block):
        return pl.ds(pl.multiple_of(block * 256, 256), 256)

    def fetch_own(block, carry):
        own = feat.at[:, :, columns(block, y)]
        pltpu.make_async_copy(own, a_ref.at[y, t, :, :, place(block)], loc_sem.at[0]).start()
        return carry

    lax.fori_loop(0, NZ, fetch_own, 0)
    fetch(images_hbm, images, loc_sem.at[1])
    fetch(counts_hbm, counts, loc_sem.at[2])
    for kind in range(2):
        fetch(kvw.at[kind, pl.ds(0, 128), :], w_ref.at[kind, z, pl.ds(0, 128), :], loc_sem.at[3 + kind])
        fetch(kvw.at[kind, third[0], :], w_ref.at[kind, z, third[0], :], loc_sem.at[5 + kind])
    q_rows = pl.ds(pl.multiple_of(slot * 192, 64), 192)
    fetch(queries.at[q_rows, pl.ds(pl.multiple_of(y * 1024, 1024), 1024)], q_ref, loc_sem.at[7])
    fetch(out_w, ow_ref, loc_sem.at[8])

    barrier = pltpu.get_barrier_semaphore()
    partners = [sibling] + [to_y(d) for d in (1, 2, 3)] + [to_x(d) for d in (1, 2, 3)]
    partners += [to_z(d) for d in (1, 2, 4, 6, 7)]
    for where in partners:
        pl.semaphore_signal(barrier, inc=1, device_id=where, device_id_type=MESH)
    pl.semaphore_wait(barrier, len(partners))

    def w_parts(s, way):
        if s < 4:
            return (pl.ds(0, 128), third[0])
        return (pl.ds(64 * way, 64), third[1 + way])

    def w_step(kind, s):
        for way, sign in ((0, -1), (1, 1)):
            origin = zm(sign * (s - 1))
            for part, rows in enumerate(w_parts(s, way)):
                src = kvw.at[kind, rows, :] if s == 1 else w_ref.at[kind, origin, rows, :]
                k = (kind * 2 + way) * 8 + (s - 1) * 2 + part
                send(src, w_ref.at[kind, origin, rows, :], w_send.at[k], w_recv.at[k], to_z(-sign))

    def w_wait(kind, s):
        for way, sign in ((0, -1), (1, 1)):
            for part, rows in enumerate(w_parts(s, way)):
                k = (kind * 2 + way) * 8 + (s - 1) * 2 + part
                arrived(w_ref.at[kind, zm(sign * s), rows, :], w_recv.at[k])

    def w_share(kind, offsets):
        for off in offsets:
            dst = w_ref.at[kind, zm(off), third[0], :]
            src = kvw.at[kind, third[0], :] if off == 0 else dst
            for d in (2, 1, 3):
                remote(src, dst, wx_send.at[kind, d - 1], wx_recv.at[kind, d - 1], to_x(d)).start()

    def w_shared(kind):
        for d in (1, 2, 3):
            rows = pl.ds(pl.multiple_of(128 + xm(-d) * 32, 32), 32)
            arrived(w_ref.at[kind, :, rows, :], wx_recv.at[kind, d - 1])

    def start_image(image):
        def start(block, carry):
            for d in (2, 1, 3):
                remote(
                    feat.at[image, :, columns(block, ym(d))], a_ref.at[y, t, image, :, place(block)],
                    f_send.at[image, d - 1], f_recv.at[image, d - 1], to_y(d),
                ).start()
            return carry

        lax.fori_loop(0, NZ, start, 0)

    def start_own(block, carry):
        own = feat.at[:, :, columns(block, y)]
        remote(own, a_ref.at[y, t, :, :, place(block)], c_fsend.at[6], c_frecv.at[6], sibling).start()
        return carry

    def pass_image(image):
        for d in (1, 2, 3):
            block = a_ref.at[ym(-d), t, image]
            arrived(block, f_recv.at[image, d - 1])
            k = image * 3 + d - 1
            send(block, block, c_fsend.at[k], c_frecv.at[k], sibling)

    w_step(0, 1)
    start_image(0)
    w_share(0, (0,))
    w_step(1, 1)
    start_image(1)
    w_share(1, (0,))
    lax.fori_loop(0, NZ, start_own, 0)

    for s in (1, 2, 3):
        for kind in range(2):
            w_wait(kind, s)
            w_step(kind, s + 1)
            w_share(kind, (-s, s))
        if s == 2:
            pass_image(0)
    w_wait(0, 4)
    w_share(0, (4,))
    w_wait(1, 4)
    w_share(1, (4,))
    pass_image(1)

    arrived(a_ref.at[y, t], loc_sem.at[0])
    for copy in locals_:
        copy.wait()
    arrived(a_ref.at[y, other], c_frecv.at[6])
    for image in range(2):
        for d in (1, 2, 3):
            arrived(a_ref.at[ym(-d), other, image], c_frecv.at[image * 3 + d - 1])

    def project(kind):
        def rows_of(src, carry):
            part = jnp.dot(
                a_ref[src].reshape(256, 2048), w_ref[kind].reshape(2048, 512), preferred_element_type=F32
            ).astype(BF)
            for core in range(2):
                for image in range(2):
                    rows = part[core * 128 + image * 64 : core * 128 + image * 64 + 64]
                    where = pl.ds(pl.multiple_of(src * 128 + core * 64, 64), 64)
                    for head in range(4):
                        p_ref[kind, head, image, where, :] = rows[:, head * 128 : head * 128 + 128]
            return carry

        lax.fori_loop(0, NY, rows_of, 0)

    def rs_start(kind):
        ss, rr = rs_send, rs_rsem
        send(p_ref.at[kind, ym(2), 0], rs_relay.at[kind, 0], ss.at[kind, 0], rr.at[kind, 0], to_y(1))
        send(p_ref.at[kind, ym(2), 1], rs_relay.at[kind, 1], ss.at[kind, 1], rr.at[kind, 1], to_y(-1))
        send(p_ref.at[kind, ym(1), 1], rs_recv.at[kind, 0, 1], ss.at[kind, 2], rr.at[kind, 2], to_y(1))
        send(p_ref.at[kind, ym(-1), 0], rs_recv.at[kind, 1, 0], ss.at[kind, 3], rr.at[kind, 3], to_y(-1))

    def rs_middle(kind):
        ss, rr = rs_send, rs_rsem
        for way, d in ((0, 1), (1, -1)):
            arrived(rs_relay.at[kind, way], rr.at[kind, way])
            p_ref[kind, ym(d), way] = (
                p_ref[kind, ym(d), way].astype(F32) + rs_relay[kind, way].astype(F32)
            ).astype(BF)
            send(
                p_ref.at[kind, ym(d), way], rs_recv.at[kind, way, way],
                ss.at[kind, 4 + way], rr.at[kind, 4 + way], to_y(d),
            )

    def rs_finish(kind):
        rr = rs_rsem
        xr_ref = (xk_ref, xv_ref)[kind]
        arrived(rs_recv.at[kind, 0, 1], rr.at[kind, 2])
        arrived(rs_recv.at[kind, 1, 0], rr.at[kind, 3])
        arrived(rs_recv.at[kind, 0, 0], rr.at[kind, 4])
        arrived(rs_recv.at[kind, 1, 1], rr.at[kind, 5])
        both = []
        for image in range(2):
            total = (
                p_ref[kind, y, image].astype(F32)
                + rs_recv[kind, 0, image].astype(F32)
                + rs_recv[kind, 1, image].astype(F32)
            )
            if kind == 0:
                mean = jnp.mean(total * total, axis=-1, keepdims=True)
                total = total * lax.rsqrt(mean + 1e-05) * gain[...]
            both.append(total.astype(BF))
        for d in (2, 1, 3, 0):
            group = xm(d)
            second = (images[0, group] == 2 * x + 1) | (images[1, group] == 2 * x + 1)
            block = jnp.where(second, both[1], both[0])
            if d == 0:
                xr_ref[x] = block
            else:
                xs_ref[kind, d - 1] = block
                send(xs_ref.at[kind, d - 1], xr_ref.at[x], x_send.at[kind, d - 1], x_recv.at[kind, d - 1], to_x(d))

    def pair(kind):
        xr_ref = (xk_ref, xv_ref)[kind]
        out_ref = (ks_ref, vs_ref)[kind]
        both_ref = (kb_ref, vb_ref)[kind]
        for d in range(1, NX):
            arrived(xr_ref.at[xm(-d)], x_recv.at[kind, d - 1])
        out_ref[...] = xr_ref[images[1 - slot, x] // 2]
        send(out_ref, both_ref.at[pl.ds(512, 512)], pair_send.at[kind], pair_recv.at[kind], partner)
        both_ref[0:512] = xr_ref[images[slot, x] // 2]

    def paired(kind):
        both_ref = (kb_ref, vb_ref)[kind]
        arrived(both_ref.at[pl.ds(512, 512)], pair_recv.at[kind])

    w_shared(0)
    project(0)
    rs_start(0)
    w_shared(1)
    project(1)
    rs_start(1)
    rs_middle(0)
    rs_middle(1)
    rs_finish(0)
    pair(0)
    rs_finish(1)
    paired(0)

    image = images[slot, x]
    scale = 1.0 / math.sqrt(HD)
    lane = lax.broadcasted_iota(jnp.int32, (192, 128), 1)
    key_row = (lax.broadcasted_iota(jnp.int32, (192, 1024), 1) + slot * 512) % 1024
    valid = key_row < counts[z // 2, image]

    def score_head(head, stats):
        q = q_ref[:, pl.ds(pl.multiple_of(head * 128, 128), 128)]
        s = lax.dot_general(q, kb_ref[...], (((1,), (1,)), ((), ())), preferred_element_type=F32) * scale
        s = jnp.where(valid, s, -1e30)
        peak = jnp.max(s, axis=-1, keepdims=True)
        e = jnp.exp(s - peak)
        total = jnp.sum(e, axis=-1, keepdims=True)
        pr_ref[head] = e.astype(BF)
        return jnp.where(lane == head, peak, jnp.where(lane == head + 8, total, stats))

    st_ref[...] = lax.fori_loop(0, 8, score_head, jnp.zeros((192, 128), F32))

    def share_of(d):
        return pl.ds(pl.multiple_of(zm(d) // 2 * 48, 16), 48)

    for k, d in enumerate((2, 4, 6)):
        send(st_ref.at[share_of(d), :], zs_ref.at[k + 1], zs_send.at[k], zs_recv.at[k], to_z(d))
    zs_ref[0] = st_ref[share_of(0), :]

    pair(1)
    paired(1)

    def weigh_head(head, carry):
        o = jnp.dot(pr_ref[head], vb_ref[...], preferred_element_type=F32)
        o_ref[:, pl.ds(pl.multiple_of(head * 128, 128), 128)] = o.astype(BF)
        return carry

    lax.fori_loop(0, 8, weigh_head, 0)
    for k, d in enumerate((2, 4, 6)):
        send(o_ref.at[share_of(d), :], zo_ref.at[k + 1], zo_send.at[k], zo_recv.at[k], to_z(d))
    zo_ref[0] = o_ref[share_of(0), :]
    for k in range(3):
        arrived(zs_ref.at[k + 1], zs_recv.at[k])
    stats = [zs_ref[k] for k in range(4)]
    peak = jnp.maximum(jnp.maximum(stats[0], stats[1]), jnp.maximum(stats[2], stats[3]))
    shares = [jnp.exp(s - peak) for s in stats]
    total = jnp.zeros((48, 128), F32)
    for k in range(4):
        total = total + shares[k] * pltpu.roll(stats[k], 120, 1)
    for k in range(3):
        arrived(zo_ref.at[k + 1], zo_recv.at[k])
    for head in range(8):
        sums = jnp.zeros((48, 128), F32)
        for k in range(4):
            sums = sums + zo_ref[k, :, head * 128 : head * 128 + 128].astype(F32) * shares[k][:, head : head + 1]
        done = (sums / total[:, head : head + 1]).astype(BF)
        if head * 128 < WIDE:
            at1[y, z, :, head * 128 : head * 128 + 128] = done
        else:
            at2[z, y, :, head * 128 - WIDE : head * 128 - WIDE + 128] = done

    def z1_step(s):
        for way, sign in ((0, -1), (1, 1)):
            if s < 4 or way == 0:
                block = at1.at[y, zm(sign * (s - 1))]
                send(block, block, z1_send.at[way, s - 1], z1_recv.at[way, s - 1], to_z(-sign))

    def z1_wait(s):
        for way, sign in ((0, -1), (1, 1)):
            if s < 4 or way == 0:
                arrived(at1.at[y, zm(sign * s)], z1_recv.at[way, s - 1])

    def z2_step(s, c):
        for way, sign in ((0, -1), (1, 1)):
            if s < 4 or way == c % 2:
                block = at2.at[zm(sign * (s - 1)), ym(-c)]
                k = (c * 2 + way) * 4 + s - 1
                send(block, block, z2_send.at[k], z2_recv.at[k], to_z(-sign))

    def z2_wait(s, c):
        for way, sign in ((0, -1), (1, 1)):
            if s < 4 or way == c % 2:
                k = (c * 2 + way) * 4 + s - 1
                arrived(at2.at[zm(sign * s), ym(-c)], z2_recv.at[k])

    def y1_step(offsets):
        for off in offsets:
            block = at1.at[y, zm(off)]
            for d in (2, 1, 3):
                k = (d - 1) * 8 + off + 3
                send(block, block, y1_send.at[k], y1_recv.at[k], to_y(d))

    z1_step(1)
    for d in (2, 1, 3):
        send(at2.at[z, y], at2.at[z, y], y2_send.at[d - 1], y2_recv.at[d - 1], to_y(d))
    z2_step(1, 0)
    y1_step((0,))
    for c in (1, 3, 2):
        arrived(at2.at[z, ym(-c)], y2_recv.at[c - 1])
        z2_step(1, c)
    for s in (1, 2, 3):
        z1_wait(s)
        z1_step(s + 1)
        y1_step((-s, s))
        for c in (0, 1, 3, 2):
            z2_wait(s, c)
            z2_step(s + 1, c)
    z1_wait(4)
    y1_step((4,))
    for c in (0, 1, 3, 2):
        z2_wait(4, c)
    for off in range(-3, 5):
        for d in (1, 2, 3):
            arrived(at1.at[ym(-d), zm(off)], y1_recv.at[(d - 1) * 8 + off + 3])

    acc = jnp.zeros((384, 256), F32)
    for block in range(NY):
        acc = acc + jnp.dot(
            at1[block].reshape(384, WIDE), ow_ref[block * 1024 : block * 1024 + WIDE], preferred_element_type=F32
        )
        acc = acc + jnp.dot(
            at2[:, block].reshape(384, NARROW), ow_ref[block * 1024 + WIDE : block * 1024 + 1024],
            preferred_element_type=F32,
        )
    acc_ref[...] = acc.reshape(4, 2, 48, 256)
    cs_ref[...] = acc_ref[:, other].reshape(192, 256).astype(BF)
    send(cs_ref, cr_ref, c_send, c_recv, sibling)
    mine_sum = acc_ref[:, t].reshape(192, 256)
    arrived(cr_ref, c_recv)
    out[...] = ((mine_sum + cr_ref[...].astype(F32)) * jnp.tanh(gate[...])).astype(BF)

    for copy in sends:
        copy.wait_send()
    for kind in range(2):
        for d in (1, 2, 3):
            arrived(w_ref.at[kind, :, third[0], :], wx_send.at[kind, d - 1])
            arrived(a_ref.at[y, t, kind], f_send.at[kind, d - 1])
    arrived(a_ref.at[y, t], c_fsend.at[6])


def local(features, kv_weights, key_gain, queries, out_weight, attn_gate, group_images, tile_valid):
    anywhere = pl.BlockSpec(memory_space=pl.ANY)
    vmem = pl.BlockSpec(memory_space=pltpu.VMEM)
    smem = pl.BlockSpec(memory_space=pltpu.SMEM)
    dma = pltpu.SemaphoreType.DMA
    return pl.pallas_call(
        fused,
        out_shape=jax.ShapeDtypeStruct((192, 256), BF),
        in_specs=[anywhere, anywhere, vmem, anywhere, anywhere, vmem, anywhere, anywhere],
        out_specs=vmem,
        scratch_shapes=[
            pltpu.SMEM((2, 4), jnp.int32),
            pltpu.SMEM((4, 8), jnp.int32),
            pltpu.VMEM((NY, 2, 2, 64, 2048), BF),
            pltpu.VMEM((2, NZ, 256, 512), BF),
            pltpu.VMEM((2, 4, 2, 512, HD), BF),
            pltpu.VMEM((2, 2, 512, HD), BF),
            pltpu.VMEM((2, 2, 2, 512, HD), BF),
            pltpu.VMEM((2, 3, 512, HD), BF),
            pltpu.VMEM((NX, 512, HD), BF),
            pltpu.VMEM((NX, 512, HD), BF),
            pltpu.VMEM((512, HD), BF),
            pltpu.VMEM((512, HD), BF),
            pltpu.VMEM((1024, HD), BF),
            pltpu.VMEM((1024, HD), BF),
            pltpu.VMEM((192, 1024), BF),
            pltpu.VMEM((8, 192, 1024), BF),
            pltpu.VMEM((192, 1024), BF),
            pltpu.VMEM((192, 128), F32),
            pltpu.VMEM((4, 48, 1024), BF),
            pltpu.VMEM((4, 48, 128), F32),
            pltpu.VMEM((NY, NZ, 48, WIDE), BF),
            pltpu.VMEM((NZ, NY, 48, NARROW), BF),
            pltpu.VMEM((4096, 256), BF),
            pltpu.VMEM((4, 2, 48, 256), F32),
            pltpu.VMEM((192, 256), BF),
            pltpu.VMEM((192, 256), BF),
            dma((9,)),
            dma((2, 3)), dma((2, 3)),
            dma((7,)), dma((7,)),
            dma((32,)), dma((32,)),
            dma((2, 3)), dma((2, 3)),
            dma((2, 6)), dma((2, 6)),
            dma((2, 3)), dma((2, 3)),
            dma((2,)), dma((2,)),
            dma((3,)), dma((3,)), dma((3,)), dma((3,)),
            dma((3,)), dma((3,)),
            dma((2, 4)), dma((2, 4)),
            dma((32,)), dma((32,)),
            dma((24,)), dma((24,)),
            dma, dma,
        ],
        compiler_params=pltpu.CompilerParams(
            collective_id=0, has_side_effects=True, vmem_limit_bytes=56 * 1024 * 1024
        ),
        name="fused",
    )(
        features, kv_weights, key_gain.reshape(1, HD), queries, out_weight,
        attn_gate.reshape(1, 1), group_images.T, tile_valid.T,
    )


def solution(mesh):
    placed = (
        P("group", ("img", "tensor"), None),
        P(None, "img", "tensor"),
        P(),
        P("group", "tensor"),
        P("tensor", "img"),
        P(),
        P(),
        P(),
    )
    return jax.shard_map(
        local, mesh=mesh, in_specs=placed, out_specs=P(("group", "tensor"), "img"), check_vma=False
    )
```

profile of v0, /device:TPU:1, one launch (start us, length us, event | category | flops | bytes accessed | tf_op | source)
XLA Modules:
  0.0 129.3 jit_solution(18345778358921831592)
XLA Ops:
  0.7 127.1 %fused.1 = bf16[192,256]{1,0:T(8,128)(2,1)} custom-call(bf16[2,64,8192]{2,1,0:T(8,128)(2,1)} %feat.1, bf16[2,256,512]{2,1,0:T(8,128)(2,1)} %kvw.1, f32[1,128]{1,0:T(1,128)} %bitcast.7, bf16[384,4096]{1,0:T(8,128)(2,1)} %queries.1, bf16[4096,256]{1,0:T(8,128)(2,1)} %out_w.1, f32[1,1]{1,0:T(1,128)} %bitcast.4.gate, s32[2,4]{1,0:T(2,128)} %bitcast.6, ...), custom_call_target="tpu_custom_call" | custom-call | tf_op jit(solution)/shard_map/fused/pallas_call | solution.py:425
  127.8 1.5 %copy.11 = bf16[192,256]{1,0:T(8,128)(2,1)} copy(bf16[192,256]{1,0:T(8,128)(2,1)} %fused.1) | data formatting | bytes 196608
where the time goes:
time: 129 us
  Pallas kernels  127 us (98%)
  local copies, waits for them, and re-layouts  1.54 us (1%)
    pallas_call x1, Pallas kernels, local(): pl.pallas_call(fused, out_shape=jax.ShapeDtypeStruct((192, 256), BF), in_...  127 us

commit v1 on v0

v1 whole, which is shorter than its diff:
```python
import math

import jax
import jax.numpy as jnp
from jax import lax
from jax.experimental import pallas as pl
from jax.experimental.pallas import tpu as pltpu
from jax.sharding import PartitionSpec as P

HD = 128
MESH = pl.DeviceIdType.MESH
BF = jnp.bfloat16
F32 = jnp.float32
NX, NY, NZ = 4, 4, 8
WIDE = 512
NARROW = 1024 - WIDE


def fused(
    feat, kvw, gain, queries, out_w, gate, images_hbm, counts_hbm, out,
    images, counts, a_ref, w_ref, p_ref, rs_relay, rs_recv, xs_ref, xk0_ref, xk1_ref, xv0_ref, xv1_ref, ps_ref, kb_ref, vb_ref,
    q_ref, pr_ref, o_ref, st_ref, zo_ref, zs_ref, at1, at2, ow_ref, acc_ref, cs_ref, cr_ref,
    loc_sem, f_send, f_recv, c_fsend, c_frecv, w_send, w_recv, wx_send, wx_recv,
    rs_send, rs_rsem, x_send, x_recv, pair_send, pair_recv, zo_send, zo_recv, zs_send, zs_recv,
    y2_send, y2_recv, z1_send, z1_recv, z2_send, z2_recv, y1_send, y1_recv, c_send, c_recv,
):
    x = lax.axis_index("group")
    img = lax.axis_index("img")
    t = lax.axis_index("tensor")
    z = img // NY
    y = img % NY
    other = 1 - t
    slot = z % 2

    def ym(d):
        return (y + d + NY) % NY

    def zm(d):
        return (z + d + NZ) % NZ

    def xm(d):
        return (x + d + NX) % NX

    def to_y(d):
        return {"img": z * NY + ym(d)}

    def to_z(d):
        return {"img": zm(d) * NY + y}

    def to_x(d):
        return {"group": xm(d)}

    sibling = {"tensor": other}
    partner = {"img": (z + 1 - 2 * slot) * NY + y}
    sends = []

    def remote(src, dst, ssem, rsem, where):
        return pltpu.make_async_remote_copy(
            src_ref=src, dst_ref=dst, send_sem=ssem, recv_sem=rsem,
            device_id=where, device_id_type=MESH,
        )

    def send(src, dst, ssem, rsem, where):
        copy = remote(src, dst, ssem, rsem, where)
        copy.start()
        sends.append(copy)

    def arrived(ref, sem):
        pltpu.make_async_copy(ref, ref, sem).wait()

    locals_ = []

    def fetch(src, dst, sem):
        copy = pltpu.make_async_copy(src, dst, sem)
        copy.start()
        locals_.append(copy)

    third = (
        pl.ds(pl.multiple_of(128 + x * 32, 32), 32),
        pl.ds(pl.multiple_of(128 + x * 32, 16), 16),
        pl.ds(pl.multiple_of(128 + x * 32 + 16, 16), 16),
    )

    def columns(block, kind):
        return pl.ds(pl.multiple_of((block * NY + kind) * 256, 256), 256)

    def place(block):
        return pl.ds(pl.multiple_of(block * 256, 256), 256)

    def fetch_own(block, carry):
        for half in range(2):
            own = feat.at[:, pl.ds(half * 32, 32), columns(block, y)]
            pltpu.make_async_copy(own, a_ref.at[half, y, t, :, :, place(block)], loc_sem.at[0]).start()
        return carry

    lax.fori_loop(0, NZ, fetch_own, 0)
    fetch(images_hbm, images, loc_sem.at[1])
    fetch(counts_hbm, counts, loc_sem.at[2])
    for kind in range(2):
        fetch(kvw.at[kind, pl.ds(0, 128), :], w_ref.at[kind, z, pl.ds(0, 128), :], loc_sem.at[3 + kind])
        fetch(kvw.at[kind, third[0], :], w_ref.at[kind, z, third[0], :], loc_sem.at[5 + kind])
    q_rows = pl.ds(pl.multiple_of(slot * 192, 64), 192)
    fetch(queries.at[q_rows, pl.ds(pl.multiple_of(y * 1024, 1024), 1024)], q_ref, loc_sem.at[7])
    fetch(out_w, ow_ref, loc_sem.at[8])

    barrier = pltpu.get_barrier_semaphore()
    partners = [sibling] + [to_y(d) for d in (1, 2, 3)] + [to_x(d) for d in (1, 2, 3)]
    partners += [to_z(d) for d in (1, 2, 4, 6, 7)]
    for where in partners:
        pl.semaphore_signal(barrier, inc=1, device_id=where, device_id_type=MESH)
    pl.semaphore_wait(barrier, len(partners))

    def w_parts(s, way):
        if s < 4:
            return (third[0], pl.ds(0, 64), pl.ds(64, 64))
        return (third[1 + way], pl.ds(64 * way, 64))

    def w_start(kind, s, way, part):
        rows = w_parts(s, way)[part]
        sign = 2 * way - 1
        origin = zm(sign * (s - 1))
        src = kvw.at[kind, rows, :] if s == 1 else w_ref.at[kind, origin, rows, :]
        k = ((kind * 2 + way) * 4 + s - 1) * 3 + part
        send(src, w_ref.at[kind, origin, rows, :], w_send.at[k], w_recv.at[k], to_z(-sign))

    def w_begin(kind):
        for part in range(3):
            for way in range(2):
                w_start(kind, 1, way, part)
        w_share(kind, (0,))

    def w_turn(kind, s):
        for part in range(3):
            for way in range(2):
                rows = w_parts(s, way)
                if part < len(rows):
                    k = ((kind * 2 + way) * 4 + s - 1) * 3 + part
                    arrived(w_ref.at[kind, zm((2 * way - 1) * s), rows[part], :], w_recv.at[k])
                if s < 3 or (s == 3 and (part == 0 or part == 1 + way)):
                    w_start(kind, s + 1, way, min(part, 1) if s == 3 else part)
            if part == 0:
                w_share(kind, (-s, s) if s < 4 else (4,))

    def w_share(kind, offsets):
        for off in offsets:
            dst = w_ref.at[kind, zm(off), third[0], :]
            src = kvw.at[kind, third[0], :] if off == 0 else dst
            for d in (2, 1, 3):
                remote(src, dst, wx_send.at[kind, d - 1], wx_recv.at[kind, d - 1], to_x(d)).start()

    def w_shared(kind):
        for d in (1, 2, 3):
            rows = pl.ds(pl.multiple_of(128 + xm(-d) * 32, 32), 32)
            arrived(w_ref.at[kind, :, rows, :], wx_recv.at[kind, d - 1])

    def start_half(half):
        def start(block, carry):
            for d in (2, 1, 3):
                remote(
                    feat.at[:, pl.ds(half * 32, 32), columns(block, ym(d))],
                    a_ref.at[half, y, t, :, :, place(block)],
                    f_send.at[half, d - 1], f_recv.at[half, d - 1], to_y(d),
                ).start()
            return carry

        lax.fori_loop(0, NZ, start, 0)

    def start_own(block, carry):
        for half in range(2):
            own = feat.at[:, pl.ds(half * 32, 32), columns(block, y)]
            remote(own, a_ref.at[half, y, t, :, :, place(block)], c_fsend.at[6], c_frecv.at[6], sibling).start()
        return carry

    def pass_half(half):
        for d in (1, 2, 3):
            block = a_ref.at[half, ym(-d), t]
            arrived(block, f_recv.at[half, d - 1])
            k = half * 3 + d - 1
            send(block, block, c_fsend.at[k], c_frecv.at[k], sibling)

    def project(kind, half, core):
        rows = a_ref[half, :, core].reshape(256, 2048)
        part = jnp.dot(rows, w_ref[kind].reshape(2048, 512), preferred_element_type=F32).astype(BF)
        for src in range(4):
            for image in range(2):
                first = src * 64 + image * 32
                where = pl.ds(pl.multiple_of(src * 64 + core * 32, 32), 32)
                for head in range(4):
                    p_ref[kind, half, head, image, where, :] = part[first : first + 32, head * 128 : head * 128 + 128]

    def siblings_rows(half):
        if half == 0:
            arrived(a_ref.at[:, y, other], c_frecv.at[6])
        for d in (1, 2, 3):
            arrived(a_ref.at[half, ym(-d), other], c_frecv.at[half * 3 + d - 1])

    def rs_start(kind, half):
        p, ss, rr = p_ref.at[kind, half], rs_send.at[kind * 2 + half], rs_rsem.at[kind * 2 + half]
        got, via = rs_recv.at[kind, half], rs_relay.at[kind, half]
        send(p.at[ym(2), 0], via.at[0], ss.at[0], rr.at[0], to_y(1))
        send(p.at[ym(2), 1], via.at[1], ss.at[1], rr.at[1], to_y(-1))
        send(p.at[ym(1), 1], got.at[0, 1], ss.at[2], rr.at[2], to_y(1))
        send(p.at[ym(-1), 0], got.at[1, 0], ss.at[3], rr.at[3], to_y(-1))

    def rs_middle(kind, half):
        p, ss, rr = p_ref.at[kind, half], rs_send.at[kind * 2 + half], rs_rsem.at[kind * 2 + half]
        got, via = rs_recv.at[kind, half], rs_relay.at[kind, half]
        for way, d in ((0, 1), (1, -1)):
            arrived(via.at[way], rr.at[way])
            p[ym(d), way] = (p[ym(d), way].astype(F32) + via[way].astype(F32)).astype(BF)
            send(p.at[ym(d), way], got.at[way, way], ss.at[4 + way], rr.at[4 + way], to_y(d))

    x_refs = (xk0_ref, xk1_ref, xv0_ref, xv1_ref)

    def rs_finish(kind, half):
        n = kind * 2 + half
        p, rr, got, xr_ref = p_ref.at[kind, half], rs_rsem.at[n], rs_recv.at[kind, half], x_refs[n]
        arrived(got.at[0, 1], rr.at[2])
        arrived(got.at[1, 0], rr.at[3])
        arrived(got.at[0, 0], rr.at[4])
        arrived(got.at[1, 1], rr.at[5])
        both = []
        for image in range(2):
            total = p[y, image].astype(F32) + got[0, image].astype(F32) + got[1, image].astype(F32)
            if kind == 0:
                mean = jnp.mean(total * total, axis=-1, keepdims=True)
                total = total * lax.rsqrt(mean + 1e-05) * gain[...]
            both.append(total.astype(BF))
        for d in (2, 1, 3, 0):
            group = xm(d)
            second = (images[0, group] == 2 * x + 1) | (images[1, group] == 2 * x + 1)
            block = jnp.where(second, both[1], both[0])
            if d == 0:
                xr_ref[x] = block
            else:
                xs_ref[n, d - 1] = block
                send(xs_ref.at[n, d - 1], xr_ref.at[x], x_send.at[n, d - 1], x_recv.at[n, d - 1], to_x(d))

    def pair(kind, half):
        n = kind * 2 + half
        xr_ref, both_ref = x_refs[n], (kb_ref, vb_ref)[kind]
        for d in range(1, NX):
            arrived(xr_ref.at[xm(-d)], x_recv.at[n, d - 1])
        ps_ref[n] = xr_ref[images[1 - slot, x] // 2]
        send(ps_ref.at[n], both_ref.at[pl.ds(512 + half * 256, 256)], pair_send.at[n], pair_recv.at[n], partner)
        both_ref[half * 256 : half * 256 + 256] = xr_ref[images[slot, x] // 2]

    def paired(kind):
        both_ref = (kb_ref, vb_ref)[kind]
        for half in range(2):
            arrived(both_ref.at[pl.ds(512 + half * 256, 256)], pair_recv.at[kind * 2 + half])

    w_begin(0)
    start_half(0)
    start_half(1)
    lax.fori_loop(0, NZ, start_own, 0)
    w_turn(0, 1)
    w_begin(1)
    w_turn(0, 2)
    w_turn(1, 1)
    pass_half(0)
    w_turn(0, 3)
    w_turn(1, 2)
    w_turn(0, 4)
    arrived(a_ref.at[:, y, t], loc_sem.at[0])
    for copy in locals_:
        copy.wait()
    w_shared(0)
    project(0, 0, t)
    siblings_rows(0)
    project(0, 0, other)
    rs_start(0, 0)
    w_turn(1, 3)
    pass_half(1)
    rs_middle(0, 0)
    w_turn(1, 4)
    project(0, 1, t)
    siblings_rows(1)
    project(0, 1, other)
    rs_start(0, 1)
    w_shared(1)
    project(1, 0, t)
    project(1, 0, other)
    rs_start(1, 0)
    rs_finish(0, 0)
    project(1, 1, t)
    project(1, 1, other)
    rs_start(1, 1)
    rs_middle(0, 1)
    rs_middle(1, 0)
    rs_middle(1, 1)
    rs_finish(0, 1)
    pair(0, 0)
    rs_finish(1, 0)
    pair(0, 1)
    rs_finish(1, 1)
    pair(1, 0)
    paired(0)

    image = images[slot, x]
    scale = 1.0 / math.sqrt(HD)
    lane = lax.broadcasted_iota(jnp.int32, (192, 128), 1)
    spot = lax.broadcasted_iota(jnp.int32, (1, 1024), 1)
    key_row = spot // 64 % 4 * 128 + spot // 32 % 2 * 64 + spot // 256 % 2 * 32 + spot % 32
    key_row = key_row + (spot // 512 + slot) % 2 * 512
    valid = jnp.broadcast_to(key_row, (192, 1024)) < counts[z // 2, image]

    def score_head(head, stats):
        q = q_ref[:, pl.ds(pl.multiple_of(head * 128, 128), 128)]
        s = lax.dot_general(q, kb_ref[...], (((1,), (1,)), ((), ())), preferred_element_type=F32) * scale
        s = jnp.where(valid, s, -1e30)
        peak = jnp.max(s, axis=-1, keepdims=True)
        e = jnp.exp(s - peak)
        total = jnp.sum(e, axis=-1, keepdims=True)
        pr_ref[head] = e.astype(BF)
        return jnp.where(lane == head, peak, jnp.where(lane == head + 8, total, stats))

    stats = lax.fori_loop(0, 4, score_head, jnp.zeros((192, 128), F32))
    pair(1, 1)
    st_ref[...] = lax.fori_loop(4, 8, score_head, stats)

    def share_of(d):
        return pl.ds(pl.multiple_of(zm(d) // 2 * 48, 16), 48)

    for k, d in enumerate((2, 4, 6)):
        send(st_ref.at[share_of(d), :], zs_ref.at[k + 1], zs_send.at[k], zs_recv.at[k], to_z(d))
    zs_ref[0] = st_ref[share_of(0), :]

    paired(1)

    def weigh_head(head, carry):
        o = jnp.dot(pr_ref[head], vb_ref[...], preferred_element_type=F32)
        o_ref[:, pl.ds(pl.multiple_of(head * 128, 128), 128)] = o.astype(BF)
        return carry

    for half in range(2):
        lax.fori_loop(half * 4, half * 4 + 4, weigh_head, 0)
        for k, d in enumerate((2, 4, 6)):
            n = half * 3 + k
            part = o_ref.at[share_of(d), pl.ds(half * 512, 512)]
            send(part, zo_ref.at[half, k + 1], zo_send.at[n], zo_recv.at[n], to_z(d))
        zo_ref[half, 0] = o_ref[share_of(0), half * 512 : half * 512 + 512]
    for k in range(3):
        arrived(zs_ref.at[k + 1], zs_recv.at[k])
    stats = [zs_ref[k] for k in range(4)]
    peak = jnp.maximum(jnp.maximum(stats[0], stats[1]), jnp.maximum(stats[2], stats[3]))
    shares = [jnp.exp(s - peak) for s in stats]
    total = jnp.zeros((48, 128), F32)
    for k in range(4):
        total = total + shares[k] * pltpu.roll(stats[k], 120, 1)
    shares = [share / total for share in shares]

    def combine(half):
        for k in range(3):
            arrived(zo_ref.at[half, k + 1], zo_recv.at[half * 3 + k])
        for head in range(4):
            cols = pl.ds(head * 128, 128)
            h = half * 4 + head
            sums = jnp.zeros((48, 128), F32)
            for k in range(4):
                sums = sums + zo_ref[half, k, :, cols].astype(F32) * shares[k][:, h : h + 1]
            done = sums.astype(BF)
            if half == 0:
                at1[y, z, :, cols] = done
            else:
                at2[z, y, :, cols] = done

    def z1_step(s):
        for way, sign in ((0, -1), (1, 1)):
            if s < 4 or way == 0:
                block = at1.at[y, zm(sign * (s - 1))]
                send(block, block, z1_send.at[way, s - 1], z1_recv.at[way, s - 1], to_z(-sign))

    def z1_wait(s):
        for way, sign in ((0, -1), (1, 1)):
            if s < 4 or way == 0:
                arrived(at1.at[y, zm(sign * s)], z1_recv.at[way, s - 1])

    def z2_step(s, c):
        for way, sign in ((0, -1), (1, 1)):
            if s < 4 or way == c % 2:
                block = at2.at[zm(sign * (s - 1)), ym(-c)]
                k = (c * 2 + way) * 4 + s - 1
                send(block, block, z2_send.at[k], z2_recv.at[k], to_z(-sign))

    def z2_wait(s, c):
        for way, sign in ((0, -1), (1, 1)):
            if s < 4 or way == c % 2:
                k = (c * 2 + way) * 4 + s - 1
                arrived(at2.at[zm(sign * s), ym(-c)], z2_recv.at[k])

    def y1_step(offsets):
        for off in offsets:
            block = at1.at[y, zm(off)]
            for d in (2, 1, 3):
                k = (d - 1) * 8 + off + 3
                send(block, block, y1_send.at[k], y1_recv.at[k], to_y(d))

    combine(0)
    z1_step(1)
    y1_step((0,))
    combine(1)
    for d in (2, 1, 3):
        send(at2.at[z, y], at2.at[z, y], y2_send.at[d - 1], y2_recv.at[d - 1], to_y(d))
    z2_step(1, 0)
    for c in (1, 3, 2):
        arrived(at2.at[z, ym(-c)], y2_recv.at[c - 1])
        z2_step(1, c)
    for s in (1, 2, 3):
        z1_wait(s)
        z1_step(s + 1)
        y1_step((-s, s))
        for c in (0, 1, 3, 2):
            z2_wait(s, c)
            z2_step(s + 1, c)
    z1_wait(4)
    y1_step((4,))
    for c in (0, 1, 3, 2):
        z2_wait(4, c)

    acc = jnp.zeros((384, 256), F32)
    for block in range(NY):
        acc = acc + jnp.dot(
            at2[:, block].reshape(384, NARROW), ow_ref[block * 1024 + WIDE : block * 1024 + 1024],
            preferred_element_type=F32,
        )
    for d in (0, 1, 3, 2):
        if d > 0:
            for off in range(-3, 5):
                arrived(at1.at[ym(-d), zm(off)], y1_recv.at[(d - 1) * 8 + off + 3])
        rows = pl.ds(pl.multiple_of(ym(-d) * 1024, 1024), WIDE)
        acc = acc + jnp.dot(at1[ym(-d)].reshape(384, WIDE), ow_ref[rows], preferred_element_type=F32)
    acc_ref[...] = acc.reshape(4, 2, 48, 256)
    cs_ref[...] = acc_ref[:, other].reshape(192, 256).astype(BF)
    send(cs_ref, cr_ref, c_send, c_recv, sibling)
    mine_sum = acc_ref[:, t].reshape(192, 256)
    arrived(cr_ref, c_recv)
    out[...] = ((mine_sum + cr_ref[...].astype(F32)) * jnp.tanh(gate[...])).astype(BF)

    for copy in sends:
        copy.wait_send()
    for kind in range(2):
        for d in (1, 2, 3):
            arrived(w_ref.at[kind, :, third[0], :], wx_send.at[kind, d - 1])
            arrived(a_ref.at[kind, y, t], f_send.at[kind, d - 1])
    arrived(a_ref.at[:, y, t], c_fsend.at[6])


def local(features, kv_weights, key_gain, queries, out_weight, attn_gate, group_images, tile_valid):
    anywhere = pl.BlockSpec(memory_space=pl.ANY)
    vmem = pl.BlockSpec(memory_space=pltpu.VMEM)
    smem = pl.BlockSpec(memory_space=pltpu.SMEM)
    dma = pltpu.SemaphoreType.DMA
    return pl.pallas_call(
        fused,
        out_shape=jax.ShapeDtypeStruct((192, 256), BF),
        in_specs=[anywhere, anywhere, vmem, anywhere, anywhere, vmem, anywhere, anywhere],
        out_specs=vmem,
        scratch_shapes=[
            pltpu.SMEM((2, 4), jnp.int32),
            pltpu.SMEM((4, 8), jnp.int32),
            pltpu.VMEM((2, NY, 2, 2, 32, 2048), BF),
            pltpu.VMEM((2, NZ, 256, 512), BF),
            pltpu.VMEM((2, 2, 4, 2, 256, HD), BF),
            pltpu.VMEM((2, 2, 2, 256, HD), BF),
            pltpu.VMEM((2, 2, 2, 2, 256, HD), BF),
            pltpu.VMEM((4, 3, 256, HD), BF),
            pltpu.VMEM((NX, 256, HD), BF),
            pltpu.VMEM((NX, 256, HD), BF),
            pltpu.VMEM((NX, 256, HD), BF),
            pltpu.VMEM((NX, 256, HD), BF),
            pltpu.VMEM((4, 256, HD), BF),
            pltpu.VMEM((1024, HD), BF),
            pltpu.VMEM((1024, HD), BF),
            pltpu.VMEM((192, 1024), BF),
            pltpu.VMEM((8, 192, 1024), BF),
            pltpu.VMEM((192, 1024), BF),
            pltpu.VMEM((192, 128), F32),
            pltpu.VMEM((2, 4, 48, 512), BF),
            pltpu.VMEM((4, 48, 128), F32),
            pltpu.VMEM((NY, NZ, 48, WIDE), BF),
            pltpu.VMEM((NZ, NY, 48, NARROW), BF),
            pltpu.VMEM((4096, 256), BF),
            pltpu.VMEM((4, 2, 48, 256), F32),
            pltpu.VMEM((192, 256), BF),
            pltpu.VMEM((192, 256), BF),
            dma((9,)),
            dma((2, 3)), dma((2, 3)),
            dma((7,)), dma((7,)),
            dma((48,)), dma((48,)),
            dma((2, 3)), dma((2, 3)),
            dma((4, 6)), dma((4, 6)),
            dma((4, 3)), dma((4, 3)),
            dma((4,)), dma((4,)),
            dma((6,)), dma((6,)), dma((3,)), dma((3,)),
            dma((3,)), dma((3,)),
            dma((2, 4)), dma((2, 4)),
            dma((32,)), dma((32,)),
            dma((24,)), dma((24,)),
            dma, dma,
        ],
        compiler_params=pltpu.CompilerParams(
            collective_id=0, has_side_effects=True, vmem_limit_bytes=56 * 1024 * 1024
        ),
        name="fused",
    )(
        features, kv_weights, key_gain.reshape(1, HD), queries, out_weight,
        attn_gate.reshape(1, 1), group_images.T, tile_valid.T,
    )


def solution(mesh):
    placed = (
        P("group", ("img", "tensor"), None),
        P(None, "img", "tensor"),
        P(),
        P("group", "tensor"),
        P("tensor", "img"),
        P(),
        P(),
        P(),
    )
    return jax.shard_map(
        local, mesh=mesh, in_specs=placed, out_specs=P(("group", "tensor"), "img"), check_vma=False
    )
```

time: 129 us -> 113 us (0.88)
  Pallas kernels: 127 us -> 111 us
    pallas_call x1, Pallas kernels: 127 us -> 111 us  [local(): pl.pallas_call(fused, out_shape=jax.ShapeDtypeStruct((192, 256), BF), in_...]
where the time goes in v1:
time: 113 us
  Pallas kernels  111 us (98%)
  local copies, waits for them, and re-layouts  1.54 us (1%)
    pallas_call x1, Pallas kernels, local(): pl.pallas_call(fused, out_shape=jax.ShapeDtypeStruct((192, 256), BF), in_...  111 us

profile of v1, /device:TPU:1, one launch (start us, length us, event | category | flops | bytes accessed | tf_op | source)
XLA Modules:
  0.0 113.3 jit_solution(1550922014057378608)
XLA Ops:
  0.7 111.1 %fused.1 = bf16[192,256]{1,0:T(8,128)(2,1)} custom-call(bf16[2,64,8192]{2,1,0:T(8,128)(2,1)} %feat.1, bf16[2,256,512]{2,1,0:T(8,128)(2,1)} %kvw.1, f32[1,128]{1,0:T(1,128)} %bitcast.7, bf16[384,4096]{1,0:T(8,128)(2,1)} %queries.1, bf16[4096,256]{1,0:T(8,128)(2,1)} %out_w.1, f32[1,1]{1,0:T(1,128)} %bitcast.4.gate, s32[2,4]{1,0:T(2,128)} %bitcast.6, ...), custom_call_target="tpu_custom_call" | custom-call | tf_op jit(solution)/shard_map/fused/pallas_call | solution.py:454
  111.7 1.5 %copy.11 = bf16[192,256]{1,0:T(8,128)(2,1)} copy(bf16[192,256]{1,0:T(8,128)(2,1)} %fused.1) | data formatting | bytes 196608

commit v2 on v1

--- a/solution.py
+++ b/solution.py
@@ -12,17 +12,15 @@
 BF = jnp.bfloat16
 F32 = jnp.float32
 NX, NY, NZ = 4, 4, 8
-WIDE = 512
-NARROW = 1024 - WIDE
 
 
 def fused(
     feat, kvw, gain, queries, out_w, gate, images_hbm, counts_hbm, out,
     images, counts, a_ref, w_ref, p_ref, rs_relay, rs_recv, xs_ref, xk0_ref, xk1_ref, xv0_ref, xv1_ref, ps_ref, kb_ref, vb_ref,
-    q_ref, pr_ref, o_ref, st_ref, zo_ref, zs_ref, at1, at2, ow_ref, acc_ref, cs_ref, cr_ref,
+    q_ref, pr_ref, o_ref, st_ref, zo_ref, zs_ref, at_ref, ow_ref, po_ref, fr_ref,
     loc_sem, f_send, f_recv, c_fsend, c_frecv, w_send, w_recv, wx_send, wx_recv,
     rs_send, rs_rsem, x_send, x_recv, pair_send, pair_recv, zo_send, zo_recv, zs_send, zs_recv,
-    y2_send, y2_recv, z1_send, z1_recv, z2_send, z2_recv, y1_send, y1_recv, c_send, c_recv,
+    ow_send, ow_recv, g_send, g_recv, po_send, po_recv,
 ):
     x = lax.axis_index("group")
     img = lax.axis_index("img")
@@ -101,11 +99,13 @@
         fetch(kvw.at[kind, third[0], :], w_ref.at[kind, z, third[0], :], loc_sem.at[5 + kind])
     q_rows = pl.ds(pl.multiple_of(slot * 192, 64), 192)
     fetch(queries.at[q_rows, pl.ds(pl.multiple_of(y * 1024, 1024), 1024)], q_ref, loc_sem.at[7])
-    fetch(out_w, ow_ref, loc_sem.at[8])
+    mine = pl.ds(pl.multiple_of(y * 1024, 1024), 1024)
+    fetch(out_w.at[mine, :], ow_ref.at[y], loc_sem.at[8])
 
     barrier = pltpu.get_barrier_semaphore()
     partners = [sibling] + [to_y(d) for d in (1, 2, 3)] + [to_x(d) for d in (1, 2, 3)]
     partners += [to_z(d) for d in (1, 2, 4, 6, 7)]
+    partners += [{**to_y(d), **sibling} for d in (1, 2, 3)]
     for where in partners:
         pl.semaphore_signal(barrier, inc=1, device_id=where, device_id_type=MESH)
     pl.semaphore_wait(barrier, len(partners))
@@ -289,6 +289,9 @@
     rs_middle(0, 1)
     rs_middle(1, 0)
     rs_middle(1, 1)
+    for d in (2, 1, 3):
+        rows = pl.ds(pl.multiple_of(ym(d) * 1024, 1024), 1024)
+        send(out_w.at[rows, :], ow_ref.at[y], ow_send.at[d - 1], ow_recv.at[d - 1], to_y(d))
     rs_finish(0, 1)
     pair(0, 0)
     rs_finish(1, 0)
@@ -360,82 +363,77 @@
             for k in range(4):
                 sums = sums + zo_ref[half, k, :, cols].astype(F32) * shares[k][:, h : h + 1]
             done = sums.astype(BF)
-            if half == 0:
-                at1[y, z, :, cols] = done
-            else:
-                at2[z, y, :, cols] = done
-
-    def z1_step(s):
-        for way, sign in ((0, -1), (1, 1)):
-            if s < 4 or way == 0:
-                block = at1.at[y, zm(sign * (s - 1))]
-                send(block, block, z1_send.at[way, s - 1], z1_recv.at[way, s - 1], to_z(-sign))
-
-    def z1_wait(s):
-        for way, sign in ((0, -1), (1, 1)):
-            if s < 4 or way == 0:
-                arrived(at1.at[y, zm(sign * s)], z1_recv.at[way, s - 1])
-
-    def z2_step(s, c):
-        for way, sign in ((0, -1), (1, 1)):
-            if s < 4 or way == c % 2:
-                block = at2.at[zm(sign * (s - 1)), ym(-c)]
-                k = (c * 2 + way) * 4 + s - 1
-                send(block, block, z2_send.at[k], z2_recv.at[k], to_z(-sign))
-
-    def z2_wait(s, c):
-        for way, sign in ((0, -1), (1, 1)):
-            if s < 4 or way == c % 2:
-                k = (c * 2 + way) * 4 + s - 1
-                arrived(at2.at[zm(sign * s), ym(-c)], z2_recv.at[k])
-
-    def y1_step(offsets):
-        for off in offsets:
-            block = at1.at[y, zm(off)]
-            for d in (2, 1, 3):
-                k = (d - 1) * 8 + off + 3
-                send(block, block, y1_send.at[k], y1_recv.at[k], to_y(d))
+            at_ref[half, z, :, cols] = done
+
+    def gather_near(half):
+        block = at_ref.at[half, z]
+        for d in (2, 6, 1, 7):
+            send(block, block, g_send.at[half, d], g_recv.at[half, d], to_z(d))
+
+    def gather_far(half):
+        for d in (2, 6, 1, 7):
+            arrived(at_ref.at[half, zm(-d)], g_recv.at[half, d])
+        across = 2 if half == 0 else 6
+        block = at_ref.at[half, zm(-across)]
+        send(block, block, g_send.at[half, 4], g_recv.at[half, 4], to_z(across))
+        for d in (1, 7):
+            block = at_ref.at[half, zm(-2 if d == 1 else 2)]
+            k = 3 if d == 1 else 5
+            send(block, block, g_send.at[half, k], g_recv.at[half, k], to_z(d))
+
+    def gathered(half):
+        for k in (4, 3, 5):
+            arrived(at_ref.at[half, zm(-k)], g_recv.at[half, k])
+
+    keep = (z + t) % 2
+
+    def project_out(group):
+        offsets = (0, 2, -1, 1) if group == 0 else (-2, 4, -3, 3)
+        rows = [
+            jnp.concatenate([at_ref[half, zm(off)] for off in offsets], axis=0) for half in range(2)
+        ]
+        for d in (2, 1, 3, 0):
+            part = jnp.dot(rows[0], ow_ref[ym(d), 0:512], preferred_element_type=F32)
+            part = part + jnp.dot(rows[1], ow_ref[ym(d), 512:1024], preferred_element_type=F32)
+            part = part.astype(BF)
+            po_ref[group, d, 0] = part[0:96]
+            po_ref[group, d, 1] = part[96:192]
+            for core in range(2):
+                block = po_ref.at[group, d, (keep + core) % 2]
+                k = (group * 4 + d) * 2 + core
+                if d > 0:
+                    where = to_y(d) if core == 0 else {**to_y(d), **sibling}
+                    send(block, fr_ref.at[group, d, core], po_send.at[k], po_recv.at[k], where)
+                elif core == 1:
+                    send(block, fr_ref.at[group, d, core], po_send.at[k], po_recv.at[k], sibling)
+
+    def finish_out(group):
+        total = po_ref[group, 0, keep].astype(F32)
+        for d in range(4):
+            for core in range(2):
+                if d > 0 or core == 1:
+                    arrived(fr_ref.at[group, d, core], po_recv.at[(group * 4 + d) * 2 + core])
+                    total = total + fr_ref[group, d, core].astype(F32)
+        total = (total * jnp.tanh(gate[...])).astype(BF)
+        for i in range(2):
+            off = 2 * i - keep if group == 0 else 6 * i - 2 - keep
+            rows = pl.ds(pl.multiple_of(zm(off) // 2 * 48, 16), 48)
+            out[rows, :] = total[i * 48 : i * 48 + 48]
 
     combine(0)
-    z1_step(1)
-    y1_step((0,))
+    gather_near(0)
     combine(1)
-    for d in (2, 1, 3):
-        send(at2.at[z, y], at2.at[z, y], y2_send.at[d - 1], y2_recv.at[d - 1], to_y(d))
-    z2_step(1, 0)
-    for c in (1, 3, 2):
-        arrived(at2.at[z, ym(-c)], y2_recv.at[c - 1])
-        z2_step(1, c)
-    for s in (1, 2, 3):
-        z1_wait(s)
-        z1_step(s + 1)
-        y1_step((-s, s))
-        for c in (0, 1, 3, 2):
-            z2_wait(s, c)
-            z2_step(s + 1, c)
-    z1_wait(4)
-    y1_step((4,))
-    for c in (0, 1, 3, 2):
-        z2_wait(4, c)
-
-    acc = jnp.zeros((384, 256), F32)
-    for block in range(NY):
-        acc = acc + jnp.dot(
-            at2[:, block].reshape(384, NARROW), ow_ref[block * 1024 + WIDE : block * 1024 + 1024],
-            preferred_element_type=F32,
-        )
-    for d in (0, 1, 3, 2):
-        if d > 0:
-            for off in range(-3, 5):
-                arrived(at1.at[ym(-d), zm(off)], y1_recv.at[(d - 1) * 8 + off + 3])
-        rows = pl.ds(pl.multiple_of(ym(-d) * 1024, 1024), WIDE)
-        acc = acc + jnp.dot(at1[ym(-d)].reshape(384, WIDE), ow_ref[rows], preferred_element_type=F32)
-    acc_ref[...] = acc.reshape(4, 2, 48, 256)
-    cs_ref[...] = acc_ref[:, other].reshape(192, 256).astype(BF)
-    send(cs_ref, cr_ref, c_send, c_recv, sibling)
-    mine_sum = acc_ref[:, t].reshape(192, 256)
-    arrived(cr_ref, c_recv)
-    out[...] = ((mine_sum + cr_ref[...].astype(F32)) * jnp.tanh(gate[...])).astype(BF)
+    gather_near(1)
+    gather_far(0)
+    gather_far(1)
+    for d in (1, 2, 3):
+        arrived(ow_ref.at[ym(-d)], ow_recv.at[d - 1])
+    project_out(0)
+    gathered(0)
+    gathered(1)
+    project_out(1)
+    finish_out(0)
+    finish_out(1)
 
     for copy in sends:
         copy.wait_send()
@@ -478,12 +476,10 @@
             pltpu.VMEM((192, 128), F32),
             pltpu.VMEM((2, 4, 48, 512), BF),
             pltpu.VMEM((4, 48, 128), F32),
-            pltpu.VMEM((NY, NZ, 48, WIDE), BF),
-            pltpu.VMEM((NZ, NY, 48, NARROW), BF),
-            pltpu.VMEM((4096, 256), BF),
-            pltpu.VMEM((4, 2, 48, 256), F32),
-            pltpu.VMEM((192, 256), BF),
-            pltpu.VMEM((192, 256), BF),
+            pltpu.VMEM((2, NZ, 48, 512), BF),
+            pltpu.VMEM((NY, 1024, 256), BF),
+            pltpu.VMEM((2, 4, 2, 96, 256), BF),
+            pltpu.VMEM((2, 4, 2, 96, 256), BF),
             dma((9,)),
             dma((2, 3)), dma((2, 3)),
             dma((7,)), dma((7,)),
@@ -494,10 +490,8 @@
             dma((4,)), dma((4,)),
             dma((6,)), dma((6,)), dma((3,)), dma((3,)),
             dma((3,)), dma((3,)),
-            dma((2, 4)), dma((2, 4)),
-            dma((32,)), dma((32,)),
-            dma((24,)), dma((24,)),
-            dma, dma,
+            dma((2, 8)), dma((2, 8)),
+            dma((16,)), dma((16,)),
         ],
         compiler_params=pltpu.CompilerParams(
             collective_id=0, has_side_effects=True, vmem_limit_bytes=56 * 1024 * 1024

time: 113 us -> 110 us (0.973)
  Pallas kernels: 111 us -> 107 us
    pallas_call x1, Pallas kernels: 111 us -> 107 us  [local(): pl.pallas_call(fused, out_shape=jax.ShapeDtypeStruct((192, 256), BF), in_...]
where the time goes in v2:
time: 110 us; the launch traced here: 109 us
  Pallas kernels  107 us (97%)
  local copies, waits for them, and re-layouts  1.54 us (1%)
    pallas_call x1, Pallas kernels, local(): pl.pallas_call(fused, out_shape=jax.ShapeDtypeStruct((192, 256), BF), in_...  107 us

profile of v2, /device:TPU:1, one launch (start us, length us, event | category | flops | bytes accessed | tf_op | source)
XLA Modules:
  0.0 109.4 jit_solution(1244657468350927804)
XLA Ops:
  0.7 107.2 %fused.1 = bf16[192,256]{1,0:T(8,128)(2,1)} custom-call(bf16[2,64,8192]{2,1,0:T(8,128)(2,1)} %feat.1, bf16[2,256,512]{2,1,0:T(8,128)(2,1)} %kvw.1, f32[1,128]{1,0:T(1,128)} %bitcast.7, bf16[384,4096]{1,0:T(8,128)(2,1)} %queries.1, bf16[4096,256]{1,0:T(8,128)(2,1)} %out_w.1, f32[1,1]{1,0:T(1,128)} %bitcast.4.gate, s32[2,4]{1,0:T(2,128)} %bitcast.6, ...), custom_call_target="tpu_custom_call" | custom-call | tf_op jit(solution)/shard_map/fused/pallas_call | solution.py:452
  107.9 1.5 %copy.11 = bf16[192,256]{1,0:T(8,128)(2,1)} copy(bf16[192,256]{1,0:T(8,128)(2,1)} %fused.1) | data formatting | bytes 196608

commit v3 on v2

--- a/solution.py
+++ b/solution.py
@@ -179,14 +179,19 @@
             send(block, block, c_fsend.at[k], c_frecv.at[k], sibling)
 
     def project(kind, half, core):
-        rows = a_ref[half, :, core].reshape(256, 2048)
+        rows = (a_ref[half] if core is None else a_ref[half, :, core]).reshape(-1, 2048)
         part = jnp.dot(rows, w_ref[kind].reshape(2048, 512), preferred_element_type=F32).astype(BF)
         for src in range(4):
             for image in range(2):
-                first = src * 64 + image * 32
-                where = pl.ds(pl.multiple_of(src * 64 + core * 32, 32), 32)
+                if core is None:
+                    both = [part[src * 128 + c * 64 + image * 32 : src * 128 + c * 64 + image * 32 + 32] for c in range(2)]
+                    rows = jnp.concatenate(both, axis=0)
+                    where = pl.ds(src * 64, 64)
+                else:
+                    rows = part[src * 64 + image * 32 : src * 64 + image * 32 + 32]
+                    where = pl.ds(pl.multiple_of(src * 64 + core * 32, 32), 32)
                 for head in range(4):
-                    p_ref[kind, half, head, image, where, :] = part[first : first + 32, head * 128 : head * 128 + 128]
+                    p_ref[kind, half, head, image, where, :] = rows[:, head * 128 : head * 128 + 128]
 
     def siblings_rows(half):
         if half == 0:
@@ -279,24 +284,22 @@
     project(0, 1, other)
     rs_start(0, 1)
     w_shared(1)
-    project(1, 0, t)
-    project(1, 0, other)
+    project(1, 0, None)
     rs_start(1, 0)
     rs_finish(0, 0)
-    project(1, 1, t)
-    project(1, 1, other)
+    project(1, 1, None)
     rs_start(1, 1)
     rs_middle(0, 1)
     rs_middle(1, 0)
     rs_middle(1, 1)
-    for d in (2, 1, 3):
-        rows = pl.ds(pl.multiple_of(ym(d) * 1024, 1024), 1024)
-        send(out_w.at[rows, :], ow_ref.at[y], ow_send.at[d - 1], ow_recv.at[d - 1], to_y(d))
     rs_finish(0, 1)
     pair(0, 0)
     rs_finish(1, 0)
     pair(0, 1)
     rs_finish(1, 1)
+    for d in (2, 1, 3):
+        rows = pl.ds(pl.multiple_of(ym(d) * 1024, 1024), 1024)
+        send(out_w.at[rows, :], ow_ref.at[y], ow_send.at[d - 1], ow_recv.at[d - 1], to_y(d))
     pair(1, 0)
     paired(0)
 

time: 110 us -> 104 us (0.945)
  Pallas kernels: 107 us -> 102 us
    pallas_call x1, Pallas kernels: 107 us -> 102 us  [local(): pl.pallas_call(fused, out_shape=jax.ShapeDtypeStruct((192, 256), BF), in_...]
where the time goes in v3:
time: 104 us
  Pallas kernels  102 us (98%)
  local copies, waits for them, and re-layouts  1.54 us (1%)
    pallas_call x1, Pallas kernels, local(): pl.pallas_call(fused, out_shape=jax.ShapeDtypeStruct((192, 256), BF), in_...  102 us

profile of v3, /device:TPU:1, one launch (start us, length us, event | category | flops | bytes accessed | tf_op | source)
XLA Modules:
  0.0 103.9 jit_solution(4531258406720843699)
XLA Ops:
  0.7 101.7 %fused.1 = bf16[192,256]{1,0:T(8,128)(2,1)} custom-call(bf16[2,64,8192]{2,1,0:T(8,128)(2,1)} %feat.1, bf16[2,256,512]{2,1,0:T(8,128)(2,1)} %kvw.1, f32[1,128]{1,0:T(1,128)} %bitcast.7, bf16[384,4096]{1,0:T(8,128)(2,1)} %queries.1, bf16[4096,256]{1,0:T(8,128)(2,1)} %out_w.1, f32[1,1]{1,0:T(1,128)} %bitcast.4.gate, s32[2,4]{1,0:T(2,128)} %bitcast.6, ...), custom_call_target="tpu_custom_call" | custom-call | tf_op jit(solution)/shard_map/fused/pallas_call | solution.py:455
  102.3 1.5 %copy.11 = bf16[192,256]{1,0:T(8,128)(2,1)} copy(bf16[192,256]{1,0:T(8,128)(2,1)} %fused.1) | data formatting | bytes 196608

commit v4 on v3

--- a/solution.py
+++ b/solution.py
@@ -51,6 +51,7 @@
     sibling = {"tensor": other}
     partner = {"img": (z + 1 - 2 * slot) * NY + y}
     sends = []
+    weight_sends = []
 
     def remote(src, dst, ssem, rsem, where):
         return pltpu.make_async_remote_copy(
@@ -63,6 +64,11 @@
         copy.start()
         sends.append(copy)
 
+    def drain(copies):
+        for copy in copies:
+            copy.wait_send()
+        copies.clear()
+
     def arrived(ref, sem):
         pltpu.make_async_copy(ref, ref, sem).wait()
 
@@ -84,6 +90,13 @@
 
     def place(block):
         return pl.ds(pl.multiple_of(block * 256, 256), 256)
+
+    barrier = pltpu.get_barrier_semaphore()
+    partners = [sibling] + [to_y(d) for d in (1, 2, 3)] + [to_x(d) for d in (1, 2, 3)]
+    partners += [to_z(d) for d in (1, 2, 4, 6, 7)]
+    partners += [{**to_y(d), **sibling} for d in (1, 2, 3)]
+    for where in partners:
+        pl.semaphore_signal(barrier, inc=1, device_id=where, device_id_type=MESH)
 
     def fetch_own(block, carry):
         for half in range(2):
@@ -102,12 +115,6 @@
     mine = pl.ds(pl.multiple_of(y * 1024, 1024), 1024)
     fetch(out_w.at[mine, :], ow_ref.at[y], loc_sem.at[8])
 
-    barrier = pltpu.get_barrier_semaphore()
-    partners = [sibling] + [to_y(d) for d in (1, 2, 3)] + [to_x(d) for d in (1, 2, 3)]
-    partners += [to_z(d) for d in (1, 2, 4, 6, 7)]
-    partners += [{**to_y(d), **sibling} for d in (1, 2, 3)]
-    for where in partners:
-        pl.semaphore_signal(barrier, inc=1, device_id=where, device_id_type=MESH)
     pl.semaphore_wait(barrier, len(partners))
 
     def w_parts(s, way):
@@ -275,8 +282,8 @@
     siblings_rows(0)
     project(0, 0, other)
     rs_start(0, 0)
+    pass_half(1)
     w_turn(1, 3)
-    pass_half(1)
     rs_middle(0, 0)
     w_turn(1, 4)
     project(0, 1, t)
@@ -286,20 +293,17 @@
     w_shared(1)
     project(1, 0, None)
     rs_start(1, 0)
-    rs_finish(0, 0)
     project(1, 1, None)
     rs_start(1, 1)
+    rs_finish(0, 0)
     rs_middle(0, 1)
     rs_middle(1, 0)
     rs_middle(1, 1)
     rs_finish(0, 1)
     pair(0, 0)
     rs_finish(1, 0)
+    rs_finish(1, 1)
     pair(0, 1)
-    rs_finish(1, 1)
-    for d in (2, 1, 3):
-        rows = pl.ds(pl.multiple_of(ym(d) * 1024, 1024), 1024)
-        send(out_w.at[rows, :], ow_ref.at[y], ow_send.at[d - 1], ow_recv.at[d - 1], to_y(d))
     pair(1, 0)
     paired(0)
 
@@ -321,9 +325,13 @@
         pr_ref[head] = e.astype(BF)
         return jnp.where(lane == head, peak, jnp.where(lane == head + 8, total, stats))
 
-    stats = lax.fori_loop(0, 4, score_head, jnp.zeros((192, 128), F32))
     pair(1, 1)
-    st_ref[...] = lax.fori_loop(4, 8, score_head, stats)
+    for d in (2, 1, 3):
+        rows = pl.ds(pl.multiple_of(ym(d) * 1024, 1024), 1024)
+        copy = remote(out_w.at[rows, :], ow_ref.at[y], ow_send.at[d - 1], ow_recv.at[d - 1], to_y(d))
+        copy.start()
+        weight_sends.append(copy)
+    st_ref[...] = lax.fori_loop(0, 8, score_head, jnp.zeros((192, 128), F32))
 
     def share_of(d):
         return pl.ds(pl.multiple_of(zm(d) // 2 * 48, 16), 48)
@@ -338,6 +346,9 @@
         o = jnp.dot(pr_ref[head], vb_ref[...], preferred_element_type=F32)
         o_ref[:, pl.ds(pl.multiple_of(head * 128, 128), 128)] = o.astype(BF)
         return carry
+
+    early = list(sends)
+    sends.clear()
 
     for half in range(2):
         lax.fori_loop(half * 4, half * 4 + 4, weigh_head, 0)
@@ -346,6 +357,12 @@
             part = o_ref.at[share_of(d), pl.ds(half * 512, 512)]
             send(part, zo_ref.at[half, k + 1], zo_send.at[n], zo_recv.at[n], to_z(d))
         zo_ref[half, 0] = o_ref[share_of(0), half * 512 : half * 512 + 512]
+    drain(early)
+    for kind in range(2):
+        for d in (1, 2, 3):
+            arrived(w_ref.at[kind, :, third[0], :], wx_send.at[kind, d - 1])
+            arrived(a_ref.at[kind, y, t], f_send.at[kind, d - 1])
+    arrived(a_ref.at[:, y, t], c_fsend.at[6])
     for k in range(3):
         arrived(zs_ref.at[k + 1], zs_recv.at[k])
     stats = [zs_ref[k] for k in range(4)]
@@ -374,7 +391,7 @@
             send(block, block, g_send.at[half, d], g_recv.at[half, d], to_z(d))
 
     def gather_far(half):
-        for d in (2, 6, 1, 7):
+        for d in (2, 6):
             arrived(at_ref.at[half, zm(-d)], g_recv.at[half, d])
         across = 2 if half == 0 else 6
         block = at_ref.at[half, zm(-across)]
@@ -431,20 +448,21 @@
     gather_far(1)
     for d in (1, 2, 3):
         arrived(ow_ref.at[ym(-d)], ow_recv.at[d - 1])
+    for half in range(2):
+        for d in (1, 7):
+            arrived(at_ref.at[half, zm(-d)], g_recv.at[half, d])
     project_out(0)
+    early = list(sends)
+    sends.clear()
     gathered(0)
     gathered(1)
     project_out(1)
+    drain(early)
+    drain(weight_sends)
     finish_out(0)
     finish_out(1)
 
-    for copy in sends:
-        copy.wait_send()
-    for kind in range(2):
-        for d in (1, 2, 3):
-            arrived(w_ref.at[kind, :, third[0], :], wx_send.at[kind, d - 1])
-            arrived(a_ref.at[kind, y, t], f_send.at[kind, d - 1])
-    arrived(a_ref.at[:, y, t], c_fsend.at[6])
+    drain(sends)
 
 
 def local(features, kv_weights, key_gain, queries, out_weight, attn_gate, group_images, tile_valid):

time: 104 us -> 101 us (0.971)
  Pallas kernels: 102 us -> 99 us
    pallas_call x1, Pallas kernels: 102 us -> 99 us  [local(): pl.pallas_call(fused, out_shape=jax.ShapeDtypeStruct((192, 256), BF), in_...]
where the time goes in v4:
time: 101 us
  Pallas kernels  99 us (98%)
  local copies, waits for them, and re-layouts  1.54 us (2%)
    pallas_call x1, Pallas kernels, local(): pl.pallas_call(fused, out_shape=jax.ShapeDtypeStruct((192, 256), BF), in_...  99 us

profile of v4, /device:TPU:1, one launch (start us, length us, event | category | flops | bytes accessed | tf_op | source)
XLA Modules:
  0.0 101.2 jit_solution(6967748952320295030)
XLA Ops:
  0.7 99.0 %fused.1 = bf16[192,256]{1,0:T(8,128)(2,1)} custom-call(bf16[2,64,8192]{2,1,0:T(8,128)(2,1)} %feat.1, bf16[2,256,512]{2,1,0:T(8,128)(2,1)} %kvw.1, f32[1,128]{1,0:T(1,128)} %bitcast.7, bf16[384,4096]{1,0:T(8,128)(2,1)} %queries.1, bf16[4096,256]{1,0:T(8,128)(2,1)} %out_w.1, f32[1,1]{1,0:T(1,128)} %bitcast.4.gate, s32[2,4]{1,0:T(2,128)} %bitcast.6, ...), custom_call_target="tpu_custom_call" | custom-call | tf_op jit(solution)/shard_map/fused/pallas_call | solution.py:473
  99.7 1.5 %copy.11 = bf16[192,256]{1,0:T(8,128)(2,1)} copy(bf16[192,256]{1,0:T(8,128)(2,1)} %fused.1) | data formatting | bytes 196608

commit v5 on v4

--- a/solution.py
+++ b/solution.py
@@ -325,13 +325,14 @@
         pr_ref[head] = e.astype(BF)
         return jnp.where(lane == head, peak, jnp.where(lane == head + 8, total, stats))
 
+    stats = lax.fori_loop(0, 2, score_head, jnp.zeros((192, 128), F32))
     pair(1, 1)
     for d in (2, 1, 3):
         rows = pl.ds(pl.multiple_of(ym(d) * 1024, 1024), 1024)
         copy = remote(out_w.at[rows, :], ow_ref.at[y], ow_send.at[d - 1], ow_recv.at[d - 1], to_y(d))
         copy.start()
         weight_sends.append(copy)
-    st_ref[...] = lax.fori_loop(0, 8, score_head, jnp.zeros((192, 128), F32))
+    st_ref[...] = lax.fori_loop(2, 8, score_head, stats)
 
     def share_of(d):
         return pl.ds(pl.multiple_of(zm(d) // 2 * 48, 16), 48)

time: 101 us -> 102 us (level)
  no operation moved by 1% of the time
where the time goes in v5:
time: 102 us
  Pallas kernels  99.5 us (98%)
  local copies, waits for them, and re-layouts  1.54 us (2%)
    pallas_call x1, Pallas kernels, local(): pl.pallas_call(fused, out_shape=jax.ShapeDtypeStruct((192, 256), BF), in_...  99.5 us

profile of v5, /device:TPU:1, one launch (start us, length us, event | category | flops | bytes accessed | tf_op | source)
XLA Modules:
  0.0 101.7 jit_solution(7650390583096156106)
XLA Ops:
  0.7 99.5 %fused.1 = bf16[192,256]{1,0:T(8,128)(2,1)} custom-call(bf16[2,64,8192]{2,1,0:T(8,128)(2,1)} %feat.1, bf16[2,256,512]{2,1,0:T(8,128)(2,1)} %kvw.1, f32[1,128]{1,0:T(1,128)} %bitcast.7, bf16[384,4096]{1,0:T(8,128)(2,1)} %queries.1, bf16[4096,256]{1,0:T(8,128)(2,1)} %out_w.1, f32[1,1]{1,0:T(1,128)} %bitcast.4.gate, s32[2,4]{1,0:T(2,128)} %bitcast.6, ...), custom_call_target="tpu_custom_call" | custom-call | tf_op jit(solution)/shard_map/fused/pallas_call | solution.py:474
  100.1 1.5 %copy.11 = bf16[192,256]{1,0:T(8,128)(2,1)} copy(bf16[192,256]{1,0:T(8,128)(2,1)} %fused.1) | data formatting | bytes 196608
